TPU v7x, 32 devices: a whole 2x2x4 slice. The times are simulated.
32 devices in a mesh: psg: 8 (over z, x), cen: 4 (over y, core).
Axes of the slice: x: 2, y: 2, z: 4, core: 2. Of those that a mesh axis runs over, the one named last changes fastest.
Arguments:
- passages: bfloat16 [256, 4096], P('psg'), may hold values from -8 to 8
- centroids: bfloat16 [65536, 4096], P(('psg', 'cen')), may hold values from -4 to 4
- dual_init: float32 [65536], P(('psg', 'cen')), may hold values from -8 to 8
Outputs:
- new_centroids: bfloat16 [65536, 4096], P(('psg', 'cen'))
- passage_duals: float32 [256], P('psg')
- centroid_duals: float32 [65536], P(('psg', 'cen'))
All inputs are finite; a program needn't handle non-finite values.
Results may differ from a plain program's by a relative error of at most 0.0047.
Values may be sent and summed in bfloat16 or wider, within the bound.
A program may use at most 64 MiB of HBM per device.

v0:
```python
import math

import jax
import jax.numpy as jnp
from jax import lax
from jax.sharding import PartitionSpec as P

CENTROIDS = 65536
ITERS = 3


def tile_logits(rows_block, centroids, factor):
    product = lax.dot_general(
        rows_block, centroids, (((1,), (1,)), ((), ())), preferred_element_type=jnp.float32
    )
    return product * factor


def row_logsum(shifted):
    top = lax.pmax(jnp.max(shifted, axis=1), ("psg", "cen"))
    total = lax.psum(jnp.sum(jnp.exp(shifted - top[:, None]), axis=1), ("psg", "cen"))
    return top + jnp.log(total)


def body(passages, centroids, dual_init):
    factor = 4.0 / math.sqrt(passages.shape[1])
    local_rows = passages.shape[0]
    gathered = lax.all_gather(passages, "psg", axis=0, tiled=True)
    count_rows = local_rows * lax.axis_size("psg")

    def logits_now():
        return tile_logits(gathered, centroids, factor)

    centroid_duals = dual_init
    passage_duals = jnp.zeros((count_rows,), jnp.float32)
    for number in range(ITERS):
        logits = logits_now()
        passage_duals = -math.log(count_rows) - row_logsum(logits + centroid_duals[None, :])
        column_terms = logits + passage_duals[:, None]
        column_top = jnp.max(column_terms, axis=0)
        column_sum = jnp.sum(jnp.exp(column_terms - column_top[None, :]), axis=0)
        centroid_duals = -math.log(CENTROIDS) - (column_top + jnp.log(column_sum))
    logits = logits_now()
    weight = (
        CENTROIDS * jnp.exp(logits + passage_duals[:, None] + centroid_duals[None, :])
    ).astype(jnp.bfloat16)
    summed = lax.dot_general(
        weight, gathered, (((0,), (0,)), ((), ())), preferred_element_type=jnp.float32
    )
    new_centroids = summed.astype(jnp.bfloat16)
    own_duals = lax.dynamic_slice_in_dim(
        passage_duals, lax.axis_index("psg") * local_rows, local_rows
    )
    return (new_centroids, own_duals, centroid_duals)


def solution(mesh):
    in_specs = (P("psg", None), P(("psg", "cen"), None), P(("psg", "cen")))
    out_specs = (P(("psg", "cen"), None), P("psg"), P(("psg", "cen")))
    return jax.shard_map(body, mesh=mesh, in_specs=in_specs, out_specs=out_specs, check_vma=False)
```

profile of v0, /device:TPU:0, one launch (start us, length us, event | category | flops | bytes accessed | tf_op | source)
XLA Modules:
  0.0 332.1 jit_solution(2510830844451252287)
XLA Ops:
  7.2 0.0 all-gather.2.cloned.1.call-start
  7.2 0.7 all-gather.2.cloned.1.call-update
  7.9 0.0 copy-start.1
  7.9 54.2 %all-gather.2.cloned.1.call-done = bf16[256,4096]{1,0:T(8,128)(2,1)} async-done(((bf16[32,4096]{1,0:T(8,128)(2,1)}), bf16[256,4096]{1,0:T(8,128)(2,1)}) %all-gather.2.cloned.1.call-update) | async-done | bytes 2097168 | tf_op jit(solution)/shard_map/all_gather | solution.py:28
  62.2 8.9 %add_reduce_fusion.4 = (f32[256]{0:T(256)S(1)}, f32[256,2048]{1,0:T(8,128)S(1)}) fusion(f32[2048]{0:T(1024)} %param.5, bf16[256,4096]{1,0:T(8,128)(2,1)} %all-gather.2.cloned.1.call-done, bf16[2048,4096]{1,0:T(8,128)(2,1)} %param.4), kind=kOutput, calls=%fused_computation.13 | convolution fusion | flops 4296540160 | bytes 20980736 | tf_op jit(solution)/shard_map/dot_general | solution.py:13
  71.1 39.3 %pmax.21 = f32[256]{0:T(256)S(1)} all-reduce(f32[256]{0:T(256)S(1)} %get-tuple-element.3), channel_id=1, replica_groups=mesh['psg'=8,'cen'=4] {'psg','cen'}, use_global_device_ids=true, to_apply=%region_1.0 | all-reduce | flops 256 | bytes 2048 | tf_op jit(solution)/shard_map/pmax | solution.py:20
  110.4 0.0 copy-done.1
  110.4 0.5 exponential_reduce_fusion.5
  110.8 39.9 %psum.21 = f32[256]{0:T(256)S(1)} all-reduce(f32[256]{0:T(256)S(1)} %exponential_reduce_fusion.5), channel_id=1, replica_groups=mesh['psg'=8,'cen'=4] {'psg','cen'}, use_global_device_ids=true, to_apply=%region_3.0 | all-reduce | flops 256 | bytes 2048 | tf_op jit(solution)/shard_map/psum | solution.py:21
  150.8 0.2 add_reduce_fusion.3
  151.0 0.4 exponential_reduce_fusion.4
  151.5 0.2 add_reduce_fusion.2
  151.7 40.1 %pmax.22 = f32[256]{0:T(256)S(1)} all-reduce(f32[256]{0:T(256)S(1)} %add_reduce_fusion.2), channel_id=1, replica_groups=mesh['psg'=8,'cen'=4] {'psg','cen'}, use_global_device_ids=true, to_apply=%region_7.0 | all-reduce | flops 256 | bytes 2048 | tf_op jit(solution)/shard_map/pmax | solution.py:20
  191.8 0.5 exponential_reduce_fusion.3
  192.3 39.9 %psum.22 = f32[256]{0:T(256)S(1)} all-reduce(f32[256]{0:T(256)S(1)} %exponential_reduce_fusion.3), channel_id=1, replica_groups=mesh['psg'=8,'cen'=4] {'psg','cen'}, use_global_device_ids=true, to_apply=%region_9.0 | all-reduce | flops 256 | bytes 2048 | tf_op jit(solution)/shard_map/psum | solution.py:21
  232.2 0.2 add_reduce_fusion.1
  232.4 0.4 exponential_reduce_fusion.2
  232.9 0.2 add_reduce_fusion
  233.1 40.1 %pmax.23 = f32[256]{0:T(256)S(1)} all-reduce(f32[256]{0:T(256)S(1)} %add_reduce_fusion), channel_id=1, replica_groups=mesh['psg'=8,'cen'=4] {'psg','cen'}, use_global_device_ids=true, to_apply=%region_13.0 | all-reduce | flops 256 | bytes 2048 | tf_op jit(solution)/shard_map/pmax | solution.py:20
  273.2 0.5 exponential_reduce_fusion.1
  273.7 40.1 %psum.23 = f32[256]{0:T(256)S(1)} all-reduce(f32[256]{0:T(256)S(1)} %exponential_reduce_fusion.1), channel_id=1, replica_groups=mesh['psg'=8,'cen'=4] {'psg','cen'}, use_global_device_ids=true, to_apply=%region_15.0 | all-reduce | flops 256 | bytes 2048 | tf_op jit(solution)/shard_map/psum | solution.py:21
  313.8 0.2 add_reduce_fusion.5
  314.0 0.4 exponential_reduce_fusion
  314.5 0.0 copy-start
  314.5 0.6 dynamic_slice.3
  315.1 10.2 %convolution_convert_fusion = bf16[2048,4096]{1,0:T(8,128)(2,1)} fusion(bf16[256,4096]{1,0:T(8,128)(2,1)} %all-gather.2.cloned.1.call-done, f32[256,2048]{1,0:T(8,128)S(1)} %get-tuple-element.4, f32[2048]{0:T(1024)S(1)} %add_subtract_fusion, f32[256]{0:T(256)S(1)} %add_subtract_fusion.3), kind=kOutput, calls=%fused_computation | convolution fusion | flops 4305453056 | bytes 20980736 | tf_op jit(solution)/shard_map/dot_general | solution.py:47
  325.3 0.0 copy-done
  (6 shorter events, 0.0 us)
Async XLA Ops:
  7.2 55.0 %all-gather.2.cloned.1.call-start = ((), (), s32[]{:S(2)}) async-start(), calls=%async_computation | async-start | bytes 2359296 | tf_op jit(solution)/shard_map/all_gather | solution.py:28
  7.9 102.5 %copy-start.1 = (f32[2048]{0:T(1024)S(1)}, f32[2048]{0:T(1024)}, u32[]{:S(2)}) copy-start(f32[2048]{0:T(1024)} %param.5) | copy-start | bytes 24580
  314.5 10.8 %copy-start = (f32[2048]{0:T(1024)}, f32[2048]{0:T(1024)S(1)}, u32[]{:S(2)}) copy-start(f32[2048]{0:T(1024)S(1)} %add_subtract_fusion) | copy-start | bytes 24580
Sparse Core Ops, SparseCore 0:
  10.1 51.9 all-gather.1
where the time goes:
time: 333 us; the launch traced here: 332 us
  blocking collectives  239 us (72%)
  waiting for transfers between devices  54.9 us (16%)
  matrix products  19.1 us (6%)
  between operations  14.1 us (4%)
  other arithmetic  3.88 us (1%)
    psum x3, blocking collectives, row_logsum(): lax.psum(jnp.sum(jnp.exp(shifted - top[:, None]), axis=1), ('psg', 'cen'))  120 us
    pmax x3, blocking collectives, row_logsum(): top = lax.pmax(jnp.max(shifted, axis=1), ('psg', 'cen'))  120 us
    all_gather x1, waiting for transfers between devices, body(): gathered = lax.all_gather(passages, 'psg', axis=0, tiled=True)  54.2 us
    dot_general x1, matrix products, body(): lax.dot_general(weight, gathered, (((0,), (0,)), ((), ())), preferred_ele...  10.2 us
    dot_general x1, matrix products, tile_logits(): lax.dot_general(rows_block, centroids, (((1,), (1,)), ((), ())), preferre...  8.92 us
  transfers between devices with their start and end apart: 1, of which 1 were waited for; matrix products, arithmetic and copies ran while one was open for 0% of the time, Pallas kernels for 0%

commit v1 on v0

v1 whole, which is shorter than its diff:
```python
import functools
import math

import jax
import jax.numpy as jnp
from jax import lax
from jax.experimental import pallas as pl
from jax.experimental.pallas import tpu as pltpu
from jax.sharding import PartitionSpec as P

CENTROIDS = 65536
ITERS = 3
LANES = 128
MESH = pl.DeviceIdType.MESH


def kernel(
    n_psg, n_cen,
    rows_ref, table_ref, init_ref,
    weight_ref, gathered_out, duals_ref, cen_duals_ref,
    table, gathered, logits, lane_top, lane_sum, duals_wide, cen_buf, psg_buf,
    table_sem, own_sem, spread_send, spread_recv, pass_send, pass_recv,
    cen_send, cen_recv, psg_send, psg_recv, out_sem,
):
    me_p, me_c = lax.axis_index("psg"), lax.axis_index("cen")
    local, depth = rows_ref.shape
    count, width = logits.shape
    part = depth // n_cen
    factor = 4.0 / math.sqrt(depth)
    sibling = me_c + 1 - 2 * lax.rem(me_c, 2)
    across = lax.rem(me_c + 2, n_cen)
    diagonal = lax.rem(sibling + 2, n_cen)
    order = (me_c, sibling, across, diagonal)

    def block(index):
        return pl.ds(pl.multiple_of(index * local, local), local)

    def quarter(index):
        return pl.ds(pl.multiple_of(index * part, part), part)

    def lanes(index):
        return pl.ds(pl.multiple_of(index * LANES, LANES), LANES)

    table_copies = []
    for at, which in enumerate(order):
        copy = pltpu.make_async_copy(
            table_ref.at[:, quarter(which)], table.at[:, quarter(which)], table_sem.at[at]
        )
        copy.start()
        table_copies.append(copy)
    own = pltpu.make_async_copy(rows_ref, gathered.at[block(me_p), :], own_sem)
    own.start()

    barrier = pltpu.get_barrier_semaphore()
    for step in range(1, n_psg):
        pl.semaphore_signal(
            barrier, inc=1, device_id=(lax.rem(me_p + step, n_psg), me_c), device_id_type=MESH
        )
    for step in range(1, n_cen):
        pl.semaphore_signal(
            barrier, inc=1, device_id=(me_p, lax.rem(me_c + step, n_cen)), device_id_type=MESH
        )
    pl.semaphore_wait(barrier, n_psg + n_cen - 2)

    def remote(src, dst, send, recv, to_p, to_c):
        return pltpu.make_async_remote_copy(
            src_ref=src, dst_ref=dst, send_sem=send, recv_sem=recv,
            device_id=(to_p, to_c), device_id_type=MESH,
        )

    sent = []
    spread = [None]
    for step in range(1, n_psg):
        copy = remote(
            rows_ref.at[:, quarter(me_c)], gathered.at[block(me_p), quarter(me_c)],
            spread_send.at[step], spread_recv.at[step], lax.rem(me_p + step, n_psg), me_c,
        )
        copy.start()
        spread.append(copy)
        sent.append(copy)

    def forward(step, kind, which, to_c):
        place = gathered.at[block(lax.rem(me_p - step + n_psg, n_psg)), quarter(which)]
        copy = remote(
            place, place, pass_send.at[kind, step], pass_recv.at[kind, step], me_p, to_c
        )
        copy.start()
        sent.append(copy)
        return copy

    from_sibling, from_across, from_diagonal = [None], [None], [None]
    for step in range(1, n_psg):
        spread[step].wait_recv()
        from_across.append(forward(step, 0, me_c, across))
        from_sibling.append(forward(step, 1, me_c, sibling))
        if step >= 2:
            from_across[step - 1].wait_recv()
            from_diagonal.append(forward(step - 1, 2, across, sibling))
    from_across[n_psg - 1].wait_recv()
    from_diagonal.append(forward(n_psg - 1, 2, across, sibling))

    own.wait()
    tile = min(width, 256)
    for at, which in enumerate(order):
        arrivals = ((), from_sibling[1:], (), from_diagonal[1:])[at]
        for copy in arrivals:
            copy.wait_recv()
        table_copies[at].wait()

        def multiply(number, carry, at=at, which=which):
            columns = pl.ds(pl.multiple_of(number * tile, tile), tile)
            product = lax.dot_general(
                gathered[:, quarter(which)], table[columns, quarter(which)],
                (((1,), (1,)), ((), ())), preferred_element_type=jnp.float32,
            )
            if at > 0:
                product = logits[:, columns] + product
            if at == len(order) - 1:
                product = product * factor
            logits[:, columns] = product
            return carry

        lax.fori_loop(0, width // tile, multiply, 0)
    out_copy = pltpu.make_async_copy(gathered, gathered_out, out_sem)
    out_copy.start()

    chunks = width // LANES

    def total_rows(number):
        lane_sum[...] = jnp.zeros_like(lane_sum)

        def add(chunk, carry):
            shifted = logits[:, lanes(chunk)] + cen_duals_ref[:, lanes(chunk)]
            lane_sum[...] += jnp.exp(shifted - lane_top[...])
            return carry

        lax.fori_loop(0, chunks, add, 0, unroll=2)
        tops, sums = lane_top[...].T, lane_sum[...].T
        top = jnp.max(tops, axis=0, keepdims=True)
        total = jnp.sum(sums * jnp.exp(tops - top), axis=0, keepdims=True)
        top, total = exchange(
            number, top, total, cen_buf, cen_send, cen_recv, n_cen, me_c,
            lambda step: (me_p, lax.rem(me_c + step, n_cen)),
        )
        return exchange(
            number, top, total, psg_buf, psg_send, psg_recv, n_psg, me_p,
            lambda step: (lax.rem(me_p + step, n_psg), me_c),
        )

    def exchange(number, top, total, buf, send, recv, size, me, target):
        upper = lax.broadcasted_iota(jnp.int32, (8, count), 0) < 4
        buf[number, me] = jnp.where(upper, top, total)
        copies = []
        for step in range(1, size):
            to_p, to_c = target(step)
            copy = remote(
                buf.at[number, me], buf.at[number, me],
                send.at[number, step], recv.at[number, step], to_p, to_c,
            )
            copy.start()
            copies.append(copy)
            sent.append(copy)
        for copy in copies:
            copy.wait_recv()
        tops = [buf[number, other, 0:1, :] for other in range(size)]
        sums = [buf[number, other, 4:5, :] for other in range(size)]
        top = functools.reduce(jnp.maximum, tops)
        total = functools.reduce(
            jnp.add, [value * jnp.exp(high - top) for high, value in zip(tops, sums)]
        )
        return top, total

    cen_duals_ref[...] = init_ref[...]
    lane_top[...] = jnp.full_like(lane_top, -jnp.inf)

    def first_top(chunk, carry):
        lane_top[...] = jnp.maximum(
            lane_top[...], logits[:, lanes(chunk)] + init_ref[:, lanes(chunk)]
        )
        return carry

    lax.fori_loop(0, chunks, first_top, 0, unroll=2)

    for number in range(ITERS):
        top, total = total_rows(number)
        duals = -math.log(count) - (top + jnp.log(total))
        duals_wide[...] = jnp.broadcast_to(duals, (LANES, count)).T
        last = number == ITERS - 1
        if last:
            duals_ref[...] = duals
        else:
            lane_top[...] = jnp.full_like(lane_top, -jnp.inf)

        def columns_pass(chunk, carry, last=last):
            terms = logits[:, lanes(chunk)] + duals_wide[...]
            column_top = jnp.max(terms, axis=0, keepdims=True)
            column_sum = jnp.sum(jnp.exp(terms - column_top), axis=0, keepdims=True)
            fresh = -math.log(CENTROIDS) - (column_top + jnp.log(column_sum))
            cen_duals_ref[:, lanes(chunk)] = fresh
            if last:
                weight_ref[:, lanes(chunk)] = (CENTROIDS * jnp.exp(terms + fresh)).astype(
                    jnp.bfloat16
                )
            else:
                lane_top[...] = jnp.maximum(lane_top[...], logits[:, lanes(chunk)] + fresh)
            return carry

        lax.fori_loop(0, chunks, columns_pass, 0, unroll=2)

    for copy in sent:
        copy.wait_send()
    out_copy.wait()


def body(n_psg, n_cen, passages, centroids, dual_init):
    local, depth = passages.shape
    width = centroids.shape[0]
    count = local * n_psg
    vmem = pl.BlockSpec(memory_space=pltpu.VMEM)
    anywhere = pl.BlockSpec(memory_space=pl.ANY)
    dma = pltpu.SemaphoreType.DMA
    weight, gathered, passage_duals, centroid_duals = pl.pallas_call(
        functools.partial(kernel, n_psg, n_cen),
        out_shape=(
            jax.ShapeDtypeStruct((count, width), jnp.bfloat16),
            jax.ShapeDtypeStruct((count, depth), jnp.bfloat16),
            jax.ShapeDtypeStruct((1, count), jnp.float32),
            jax.ShapeDtypeStruct((1, width), jnp.float32),
        ),
        in_specs=[vmem, anywhere, vmem],
        out_specs=(vmem, anywhere, vmem, vmem),
        scratch_shapes=[
            pltpu.VMEM((width, depth), jnp.bfloat16),
            pltpu.VMEM((count, depth), jnp.bfloat16),
            pltpu.VMEM((count, width), jnp.float32),
            pltpu.VMEM((count, LANES), jnp.float32),
            pltpu.VMEM((count, LANES), jnp.float32),
            pltpu.VMEM((count, LANES), jnp.float32),
            pltpu.VMEM((ITERS, n_cen, 8, count), jnp.float32),
            pltpu.VMEM((ITERS, n_psg, 8, count), jnp.float32),
            dma((n_cen,)),
            dma,
            dma((n_psg,)),
            dma((n_psg,)),
            dma((3, n_psg)),
            dma((3, n_psg)),
            dma((ITERS, n_cen)),
            dma((ITERS, n_cen)),
            dma((ITERS, n_psg)),
            dma((ITERS, n_psg)),
            dma,
        ],
        compiler_params=pltpu.CompilerParams(
            collective_id=0, has_side_effects=True, vmem_limit_bytes=56 * 1024 * 1024
        ),
    )(passages, centroids, dual_init.reshape(1, width))
    summed = lax.dot_general(
        weight, gathered, (((0,), (0,)), ((), ())), preferred_element_type=jnp.float32
    )
    own_duals = lax.dynamic_slice_in_dim(
        passage_duals.reshape(count), lax.axis_index("psg") * local, local
    )
    return (summed.astype(jnp.bfloat16), own_duals, centroid_duals.reshape(width))


def solution(mesh):
    in_specs = (P("psg", None), P(("psg", "cen"), None), P(("psg", "cen")))
    out_specs = (P(("psg", "cen"), None), P("psg"), P(("psg", "cen")))
    return jax.shard_map(
        functools.partial(body, mesh.shape["psg"], mesh.shape["cen"]),
        mesh=mesh, in_specs=in_specs, out_specs=out_specs, check_vma=False,
    )
```

time: 333 us -> 83.5 us (0.25)
  blocking collectives: 239 us -> 0 us
  Pallas kernels: 0 us -> 68.2 us
  waiting for transfers between devices: 54.9 us -> 0 us
  between operations: 14.1 us -> 0.65 us
  matrix products: 19.1 us -> 12.6 us
  other arithmetic: 3.88 us -> 0 us
    psum x3 -> x0, blocking collectives: 120 us -> none  [row_logsum(): lax.psum(jnp.sum(jnp.exp(shifted - top[:, None]), axis=1), ('psg', 'cen'))]
    pmax x3 -> x0, blocking collectives: 120 us -> none  [row_logsum(): top = lax.pmax(jnp.max(shifted, axis=1), ('psg', 'cen'))]
    pallas_call x0 -> x1, Pallas kernels: none -> 68.2 us  [body(): pl.pallas_call(functools.partial(kernel, n_psg, n_cen), out_shape=(jax.Sh...]
    all_gather x1 -> x0, waiting for transfers between devices: 54.2 us -> none  [body(): gathered = lax.all_gather(passages, 'psg', axis=0, tiled=True)]
    dot_general x1 -> x0, matrix products: 8.92 us -> none  [tile_logits(): lax.dot_general(rows_block, centroids, (((1,), (1,)), ((), ())), preferre...]
  transfers between devices with their start and end apart: 1 -> 0, of which waited for: 1 -> 0; matrix products, arithmetic and copies ran while one was open for 0% -> 0% of each run, Pallas kernels for 0% -> 0%
where the time goes in v1:
time: 83.5 us; the launch traced here: 83.3 us
  Pallas kernels  68.2 us (82%)
  matrix products  12.6 us (15%)
  local copies, waits for them, and re-layouts  1.8 us (2%)
    pallas_call x1, Pallas kernels, body(): pl.pallas_call(functools.partial(kernel, n_psg, n_cen), out_shape=(jax.Sh...  68.2 us
    dot_general x1, matrix products, body(): lax.dot_general(weight, gathered, (((0,), (0,)), ((), ())), preferred_ele...  12.6 us

profile of v1, /device:TPU:0, one launch (start us, length us, event | category | flops | bytes accessed | tf_op | source)
XLA Modules:
  0.0 83.3 jit_solution(8554048687861580467)
XLA Ops:
  0.6 68.2 %shard_map.58 = (bf16[256,2048]{1,0:T(8,128)(2,1)}, bf16[256,4096]{1,0:T(8,128)(2,1)}, f32[1,256]{1,0:T(1,128)}, f32[1,2048]{1,0:T(1,128)}) custom-call(bf16[32,4096]{1,0:T(8,128)(2,1)} %rows_ref.1, bf16[2048,4096]{1,0:T(8,128)(2,1)} %table_ref.1, f32[1,2048]{1,0:T(1,128)} %bitcast.6), custom_call_target="tpu_custom_call" | custom-call | tf_op jit(solution)/shard_map/pallas_call | solution.py:222
  68.9 0.0 copy-start
  68.9 1.2 %dynamic-slice_bitcast_fusion = f32[32]{0:T(128)} fusion(f32[1,256]{1,0:T(1,128)} %get-tuple-element.9, s32[]{:T(128)S(6)} %select_n.3), kind=kLoop, calls=%fused_computation.1 | loop fusion | bytes 260 | tf_op jit(solution)/shard_map/dynamic_slice | solution.py:260
  70.1 12.6 %convolution_convert_fusion = bf16[2048,4096]{1,0:T(8,128)(2,1)} fusion(bf16[256,2048]{1,0:T(8,128)(2,1)} %get-tuple-element.7, bf16[256,4096]{1,0:T(8,128)(2,1)} %get-tuple-element.8), kind=kOutput, calls=%fused_computation | convolution fusion | flops 4303355904 | bytes 19922944 | tf_op jit(solution)/shard_map/dot_general | solution.py:257
  82.7 0.0 copy-done
  82.7 0.6 copy.7
Async XLA Ops:
  68.9 13.9 %copy-start = (f32[1,2048]{1,0:T(1,128)S(1)}, f32[1,2048]{1,0:T(1,128)}, u32[]{:S(2)}) copy-start(f32[1,2048]{1,0:T(1,128)} %get-tuple-element.10) | copy-start | bytes 24580

commit v2 on v1

--- a/solution.py
+++ b/solution.py
@@ -88,26 +88,22 @@
         sent.append(copy)
         return copy
 
-    from_sibling, from_across, from_diagonal = [None], [None], [None]
+    from_sibling, from_across = [], []
     for step in range(1, n_psg):
         spread[step].wait_recv()
         from_across.append(forward(step, 0, me_c, across))
         from_sibling.append(forward(step, 1, me_c, sibling))
-        if step >= 2:
-            from_across[step - 1].wait_recv()
-            from_diagonal.append(forward(step - 1, 2, across, sibling))
-    from_across[n_psg - 1].wait_recv()
-    from_diagonal.append(forward(n_psg - 1, 2, across, sibling))
 
     own.wait()
     tile = min(width, 256)
-    for at, which in enumerate(order):
-        arrivals = ((), from_sibling[1:], (), from_diagonal[1:])[at]
+
+    def accumulate(at, arrivals):
         for copy in arrivals:
             copy.wait_recv()
         table_copies[at].wait()
-
-        def multiply(number, carry, at=at, which=which):
+        which = order[at]
+
+        def multiply(number, carry):
             columns = pl.ds(pl.multiple_of(number * tile, tile), tile)
             product = lax.dot_general(
                 gathered[:, quarter(which)], table[columns, quarter(which)],
@@ -121,6 +117,15 @@
             return carry
 
         lax.fori_loop(0, width // tile, multiply, 0)
+
+    accumulate(0, ())
+    from_diagonal = []
+    for step in range(1, n_psg):
+        from_across[step - 1].wait_recv()
+        from_diagonal.append(forward(step, 2, across, sibling))
+    accumulate(1, from_sibling)
+    accumulate(2, ())
+    accumulate(3, from_diagonal)
     out_copy = pltpu.make_async_copy(gathered, gathered_out, out_sem)
     out_copy.start()
 
@@ -210,6 +215,28 @@
     for copy in sent:
         copy.wait_send()
     out_copy.wait()
+
+
+def update_kernel(n_psg, weight_ref, gathered_ref, duals_ref, cen_ref, out_ref, own_ref, cen_out_ref):
+    depth = out_ref.shape[1]
+    local = own_ref.shape[1]
+    step = min(depth, 512)
+
+    @pl.when(pl.program_id(0) == 0)
+    def _():
+        me = lax.axis_index("psg")
+        own = duals_ref[:, 0:local]
+        for index in range(1, n_psg):
+            own = jnp.where(me == index, duals_ref[:, index * local:(index + 1) * local], own)
+        own_ref[...] = own
+        cen_out_ref[...] = cen_ref[...]
+
+    weight = weight_ref[...]
+    for start in range(0, depth, step):
+        out_ref[:, start:start + step] = lax.dot_general(
+            weight, gathered_ref[:, start:start + step], (((0,), (0,)), ((), ())),
+            preferred_element_type=jnp.float32,
+        ).astype(out_ref.dtype)
 
 
 def body(n_psg, n_cen, passages, centroids, dual_init):
@@ -254,13 +281,29 @@
             collective_id=0, has_side_effects=True, vmem_limit_bytes=56 * 1024 * 1024
         ),
     )(passages, centroids, dual_init.reshape(1, width))
-    summed = lax.dot_general(
-        weight, gathered, (((0,), (0,)), ((), ())), preferred_element_type=jnp.float32
-    )
-    own_duals = lax.dynamic_slice_in_dim(
-        passage_duals.reshape(count), lax.axis_index("psg") * local, local
-    )
-    return (summed.astype(jnp.bfloat16), own_duals, centroid_duals.reshape(width))
+    tile = min(width, 256)
+    new_centroids, own_duals, final_duals = pl.pallas_call(
+        functools.partial(update_kernel, n_psg),
+        grid=(width // tile,),
+        out_shape=(
+            jax.ShapeDtypeStruct((width, depth), jnp.bfloat16),
+            jax.ShapeDtypeStruct((1, local), jnp.float32),
+            jax.ShapeDtypeStruct((1, width), jnp.float32),
+        ),
+        in_specs=[
+            pl.BlockSpec((count, tile), lambda i: (0, i)),
+            pl.BlockSpec((count, depth), lambda i: (0, 0)),
+            pl.BlockSpec((1, count), lambda i: (0, 0)),
+            pl.BlockSpec((1, width), lambda i: (0, 0)),
+        ],
+        out_specs=(
+            pl.BlockSpec((tile, depth), lambda i: (i, 0)),
+            pl.BlockSpec((1, local), lambda i: (0, 0)),
+            pl.BlockSpec((1, width), lambda i: (0, 0)),
+        ),
+        compiler_params=pltpu.CompilerParams(vmem_limit_bytes=60 * 1024 * 1024),
+    )(weight, gathered, passage_duals, centroid_duals)
+    return (new_centroids, own_duals.reshape(local), final_duals.reshape(width))
 
 
 def solution(mesh):

time: 83.5 us -> 75.2 us (0.901)
  matrix products: 12.6 us -> 0 us
  Pallas kernels: 68.2 us -> 74.3 us
  local copies, waits for them, and re-layouts: 1.8 us -> 0 us
    dot_general x1 -> x0, matrix products: 12.6 us -> none  [body(): lax.dot_general(weight, gathered, (((0,), (0,)), ((), ())), preferred_ele...]
    pallas_call x0 -> x1, Pallas kernels: none -> 11.5 us  [body(): pl.pallas_call(functools.partial(update_kernel, n_psg), grid=(width // ti...]
    pallas_call x1, Pallas kernels: 68.2 us -> 62.8 us  [body(): pl.pallas_call(functools.partial(kernel, n_psg, n_cen), out_shape=(jax.Sh...]
    dynamic_slice x1 -> x0, local copies, waits for them, and re-layouts: 1.2 us -> none  [body(): lax.dynamic_slice_in_dim(passage_duals.reshape(count), lax.axis_index('ps...]
where the time goes in v2:
time: 75.2 us; the launch traced here: 75 us
  Pallas kernels  74.3 us (99%)
    pallas_call x1, Pallas kernels, body(): pl.pallas_call(functools.partial(kernel, n_psg, n_cen), out_shape=(jax.Sh...  62.8 us
    pallas_call x1, Pallas kernels, body(): pl.pallas_call(functools.partial(update_kernel, n_psg), grid=(width // ti...  11.5 us

profile of v2, /device:TPU:0, one launch (start us, length us, event | category | flops | bytes accessed | tf_op | source)
XLA Modules:
  0.0 75.0 jit_solution(8549065785579543383)
XLA Ops:
  0.6 62.8 %shard_map.58 = (bf16[256,2048]{1,0:T(8,128)(2,1)}, bf16[256,4096]{1,0:T(8,128)(2,1)}, f32[1,256]{1,0:T(1,128)}, f32[1,2048]{1,0:T(1,128)}) custom-call(bf16[32,4096]{1,0:T(8,128)(2,1)} %rows_ref.1, bf16[2048,4096]{1,0:T(8,128)(2,1)} %table_ref.1, f32[1,2048]{1,0:T(1,128)} %bitcast.3), custom_call_target="tpu_custom_call" | custom-call | tf_op jit(solution)/shard_map/pallas_call | solution.py:249
  63.5 11.5 %shard_map.59 = (bf16[2048,4096]{1,0:T(8,128)(2,1)}, f32[1,32]{1,0:T(1,128)}, f32[1,2048]{1,0:T(1,128)}) custom-call(bf16[256,2048]{1,0:T(8,128)(2,1)} %get-tuple-element.10.weight_ref, bf16[256,4096]{1,0:T(8,128)(2,1)} %get-tuple-element.11.gathered_ref, f32[1,256]{1,0:T(1,128)} %get-tuple-element.12.duals_ref, f32[1,2048]{1,0:T(1,128)} %get-tuple-element.13.cen_ref), custom_call_target="tpu_custom_call" | custom-call | tf_op jit(solution)/shard_map/pallas_call | solution.py:285

commit v3 on v2

--- a/solution.py
+++ b/solution.py
@@ -130,16 +130,27 @@
     out_copy.start()
 
     chunks = width // LANES
+    groups = 4 if chunks % 4 == 0 else 1
+
+    slab = min(count, 32)
 
     def total_rows(number):
-        lane_sum[...] = jnp.zeros_like(lane_sum)
-
-        def add(chunk, carry):
-            shifted = logits[:, lanes(chunk)] + cen_duals_ref[:, lanes(chunk)]
-            lane_sum[...] += jnp.exp(shifted - lane_top[...])
+        def add(index, carry):
+            rows = pl.ds(pl.multiple_of(index * slab, slab), slab)
+
+            def shifted(chunk):
+                place = slice(chunk * LANES, (chunk + 1) * LANES)
+                return logits[rows, place] + cen_duals_ref[:, place]
+
+            top = functools.reduce(jnp.maximum, [shifted(chunk) for chunk in range(chunks)])
+            total = jnp.exp(shifted(0) - top)
+            for chunk in range(1, chunks):
+                total = total + jnp.exp(shifted(chunk) - top)
+            lane_top[rows, :] = top
+            lane_sum[rows, :] = total
             return carry
 
-        lax.fori_loop(0, chunks, add, 0, unroll=2)
+        lax.fori_loop(0, count // slab, add, 0, unroll=2)
         tops, sums = lane_top[...].T, lane_sum[...].T
         top = jnp.max(tops, axis=0, keepdims=True)
         total = jnp.sum(sums * jnp.exp(tops - top), axis=0, keepdims=True)
@@ -176,16 +187,6 @@
         return top, total
 
     cen_duals_ref[...] = init_ref[...]
-    lane_top[...] = jnp.full_like(lane_top, -jnp.inf)
-
-    def first_top(chunk, carry):
-        lane_top[...] = jnp.maximum(
-            lane_top[...], logits[:, lanes(chunk)] + init_ref[:, lanes(chunk)]
-        )
-        return carry
-
-    lax.fori_loop(0, chunks, first_top, 0, unroll=2)
-
     for number in range(ITERS):
         top, total = total_rows(number)
         duals = -math.log(count) - (top + jnp.log(total))
@@ -193,24 +194,25 @@
         last = number == ITERS - 1
         if last:
             duals_ref[...] = duals
-        else:
-            lane_top[...] = jnp.full_like(lane_top, -jnp.inf)
-
-        def columns_pass(chunk, carry, last=last):
-            terms = logits[:, lanes(chunk)] + duals_wide[...]
-            column_top = jnp.max(terms, axis=0, keepdims=True)
-            column_sum = jnp.sum(jnp.exp(terms - column_top), axis=0, keepdims=True)
-            fresh = -math.log(CENTROIDS) - (column_top + jnp.log(column_sum))
-            cen_duals_ref[:, lanes(chunk)] = fresh
-            if last:
-                weight_ref[:, lanes(chunk)] = (CENTROIDS * jnp.exp(terms + fresh)).astype(
-                    jnp.bfloat16
-                )
-            else:
-                lane_top[...] = jnp.maximum(lane_top[...], logits[:, lanes(chunk)] + fresh)
+
+        def columns_pass(index, carry, last=last):
+            places = [lanes(index * groups + group) for group in range(groups)]
+            terms = [logits[:, place] + duals_wide[...] for place in places]
+            tops = [jnp.max(term, axis=0, keepdims=True) for term in terms]
+            sums = [
+                jnp.sum(jnp.exp(term - high), axis=0, keepdims=True)
+                for term, high in zip(terms, tops)
+            ]
+            for place, term, high, value in zip(places, terms, tops, sums):
+                fresh = -math.log(CENTROIDS) - (high + jnp.log(value))
+                cen_duals_ref[:, place] = fresh
+                if last:
+                    weight_ref[:, place] = (CENTROIDS * jnp.exp(term + fresh)).astype(
+                        jnp.bfloat16
+                    )
             return carry
 
-        lax.fori_loop(0, chunks, columns_pass, 0, unroll=2)
+        lax.fori_loop(0, chunks // groups, columns_pass, 0)
 
     for copy in sent:
         copy.wait_send()
@@ -231,10 +233,10 @@
         own_ref[...] = own
         cen_out_ref[...] = cen_ref[...]
 
-    weight = weight_ref[...]
+    weight = weight_ref[...].T
     for start in range(0, depth, step):
         out_ref[:, start:start + step] = lax.dot_general(
-            weight, gathered_ref[:, start:start + step], (((0,), (0,)), ((), ())),
+            weight, gathered_ref[:, start:start + step], (((1,), (0,)), ((), ())),
             preferred_element_type=jnp.float32,
         ).astype(out_ref.dtype)
 
@@ -281,7 +283,7 @@
             collective_id=0, has_side_effects=True, vmem_limit_bytes=56 * 1024 * 1024
         ),
     )(passages, centroids, dual_init.reshape(1, width))
-    tile = min(width, 256)
+    tile = min(width, 512)
     new_centroids, own_duals, final_duals = pl.pallas_call(
         functools.partial(update_kernel, n_psg),
         grid=(width // tile,),

time: 75.2 us -> 72.5 us (0.964)
  Pallas kernels: 74.3 us -> 71.7 us
    pallas_call x1, Pallas kernels: 62.8 us -> 61.4 us  [body(): pl.pallas_call(functools.partial(kernel, n_psg, n_cen), out_shape=(jax.Sh...]
    pallas_call x1, Pallas kernels: 11.5 us -> 10.2 us  [body(): pl.pallas_call(functools.partial(update_kernel, n_psg), grid=(width // ti...]
where the time goes in v3:
time: 72.5 us; the launch traced here: 72.3 us
  Pallas kernels  71.7 us (99%)
    pallas_call x1, Pallas kernels, body(): pl.pallas_call(functools.partial(kernel, n_psg, n_cen), out_shape=(jax.Sh...  61.4 us
    pallas_call x1, Pallas kernels, body(): pl.pallas_call(functools.partial(update_kernel, n_psg), grid=(width // ti...  10.2 us

profile of v3, /device:TPU:0, one launch (start us, length us, event | category | flops | bytes accessed | tf_op | source)
XLA Modules:
  0.0 72.3 jit_solution(1536786869162414862)
XLA Ops:
  0.6 61.4 %shard_map.58 = (bf16[256,2048]{1,0:T(8,128)(2,1)}, bf16[256,4096]{1,0:T(8,128)(2,1)}, f32[1,256]{1,0:T(1,128)}, f32[1,2048]{1,0:T(1,128)}) custom-call(bf16[32,4096]{1,0:T(8,128)(2,1)} %rows_ref.1, bf16[2048,4096]{1,0:T(8,128)(2,1)} %table_ref.1, f32[1,2048]{1,0:T(1,128)} %bitcast.3), custom_call_target="tpu_custom_call" | custom-call | tf_op jit(solution)/shard_map/pallas_call | solution.py:251
  62.1 10.2 %shard_map.59 = (bf16[2048,4096]{1,0:T(8,128)(2,1)}, f32[1,32]{1,0:T(1,128)}, f32[1,2048]{1,0:T(1,128)}) custom-call(bf16[256,2048]{1,0:T(8,128)(2,1)} %get-tuple-element.10.weight_ref, bf16[256,4096]{1,0:T(8,128)(2,1)} %get-tuple-element.11.gathered_ref, f32[1,256]{1,0:T(1,128)} %get-tuple-element.12.duals_ref, f32[1,2048]{1,0:T(1,128)} %get-tuple-element.13.cen_ref), custom_call_target="tpu_custom_call" | custom-call | tf_op jit(solution)/shard_map/pallas_call | solution.py:287

commit v4 on v3

--- a/solution.py
+++ b/solution.py
@@ -19,7 +19,7 @@
     rows_ref, table_ref, init_ref,
     weight_ref, gathered_out, duals_ref, cen_duals_ref,
     table, gathered, logits, lane_top, lane_sum, duals_wide, cen_buf, psg_buf,
-    table_sem, own_sem, spread_send, spread_recv, pass_send, pass_recv,
+    table_sem, own_sem, pass_send, pass_recv,
     cen_send, cen_recv, psg_send, psg_recv, out_sem,
 ):
     me_p, me_c = lax.axis_index("psg"), lax.axis_index("cen")
@@ -69,30 +69,62 @@
         )
 
     sent = []
-    spread = [None]
-    for step in range(1, n_psg):
+
+    def send(kind, row, step, rows, columns, to_p, to_c, source=None):
+        place = gathered.at[rows, columns]
         copy = remote(
-            rows_ref.at[:, quarter(me_c)], gathered.at[block(me_p), quarter(me_c)],
-            spread_send.at[step], spread_recv.at[step], lax.rem(me_p + step, n_psg), me_c,
-        )
-        copy.start()
-        spread.append(copy)
-        sent.append(copy)
-
-    def forward(step, kind, which, to_c):
-        place = gathered.at[block(lax.rem(me_p - step + n_psg, n_psg)), quarter(which)]
-        copy = remote(
-            place, place, pass_send.at[kind, step], pass_recv.at[kind, step], me_p, to_c
+            place if source is None else source, place,
+            pass_send.at[kind, row, step], pass_recv.at[kind, row, step], to_p, to_c,
         )
         copy.start()
         sent.append(copy)
         return copy
 
-    from_sibling, from_across = [], []
-    for step in range(1, n_psg):
-        spread[step].wait_recv()
-        from_across.append(forward(step, 0, me_c, across))
-        from_sibling.append(forward(step, 1, me_c, sibling))
+    pairs = n_psg // 2
+    me_z, me_x = me_p // 2, lax.rem(me_p, 2)
+    mate = me_p + 1 - 2 * me_x
+
+    def eighth(index, side):
+        return pl.ds(pl.multiple_of(index * part + side * (part // 2), part // 2), part // 2)
+
+    def pair(step):
+        index = lax.rem(me_z - step + pairs, pairs)
+        return pl.ds(pl.multiple_of(index * 2 * local, 2 * local), 2 * local)
+
+    def peer(step):
+        return lax.rem(me_z + step, pairs) * 2 + me_x
+
+    mine = eighth(me_c, me_x)
+    to_mate = [
+        send(
+            0, 0, 0, block(me_p), quarter(me_c), mate, me_c,
+            source=rows_ref.at[:, quarter(me_c)],
+        )
+    ]
+    along = [[None], [None]]
+    for step in range(1, pairs):
+        along[0].append(
+            send(1, 0, step, block(me_p), mine, peer(step), me_c, source=rows_ref.at[:, mine])
+        )
+    to_mate[0].wait_recv()
+    for step in range(1, pairs):
+        along[1].append(send(1, 1, step, block(mate), mine, peer(step), me_c))
+    pieces = [(0, 0, block(mate), None)]
+    from_across = [send(2, 0, 0, block(mate), quarter(me_c), me_p, across)]
+    from_sibling = [send(3, 0, 0, block(mate), quarter(me_c), me_p, sibling)]
+    for row in range(2):
+        side = me_x if row == 0 else 1 - me_x
+        for step in range(1, pairs):
+            if row == 0:
+                along[0][step].wait_recv()
+                along[1][step].wait_recv()
+                to_mate.append(send(0, 0, step, pair(step), mine, mate, me_c))
+            else:
+                to_mate[step].wait_recv()
+            pieces.append((row, step, pair(step), side))
+            columns = eighth(me_c, side)
+            from_across.append(send(2, row, step, pair(step), columns, me_p, across))
+            from_sibling.append(send(3, row, step, pair(step), columns, me_p, sibling))
 
     own.wait()
     tile = min(width, 256)
@@ -119,11 +151,12 @@
         lax.fori_loop(0, width // tile, multiply, 0)
 
     accumulate(0, ())
+    accumulate(1, from_sibling)
     from_diagonal = []
-    for step in range(1, n_psg):
-        from_across[step - 1].wait_recv()
-        from_diagonal.append(forward(step, 2, across, sibling))
-    accumulate(1, from_sibling)
+    for copy, (row, step, rows, side) in zip(from_across, pieces):
+        copy.wait_recv()
+        columns = quarter(across) if side is None else eighth(across, side)
+        from_diagonal.append(send(4, row, step, rows, columns, me_p, sibling))
     accumulate(2, ())
     accumulate(3, from_diagonal)
     out_copy = pltpu.make_async_copy(gathered, gathered_out, out_sem)
@@ -269,10 +302,8 @@
             pltpu.VMEM((ITERS, n_psg, 8, count), jnp.float32),
             dma((n_cen,)),
             dma,
-            dma((n_psg,)),
-            dma((n_psg,)),
-            dma((3, n_psg)),
-            dma((3, n_psg)),
+            dma((5, 2, n_psg // 2)),
+            dma((5, 2, n_psg // 2)),
             dma((ITERS, n_cen)),
             dma((ITERS, n_cen)),
             dma((ITERS, n_psg)),

time: 72.5 us -> 68.6 us (0.946)
  Pallas kernels: 71.7 us -> 67.8 us
    pallas_call x1, Pallas kernels: 61.4 us -> 57.6 us  [body(): pl.pallas_call(functools.partial(kernel, n_psg, n_cen), out_shape=(jax.Sh...]
where the time goes in v4:
time: 68.6 us; the launch traced here: 68.5 us
  Pallas kernels  67.8 us (99%)
    pallas_call x1, Pallas kernels, body(): pl.pallas_call(functools.partial(kernel, n_psg, n_cen), out_shape=(jax.Sh...  57.6 us
    pallas_call x1, Pallas kernels, body(): pl.pallas_call(functools.partial(update_kernel, n_psg), grid=(width // ti...  10.2 us

profile of v4, /device:TPU:0, one launch (start us, length us, event | category | flops | bytes accessed | tf_op | source)
XLA Modules:
  0.0 68.5 jit_solution(16486336406784915467)
XLA Ops:
  0.6 57.6 %shard_map.58 = (bf16[256,2048]{1,0:T(8,128)(2,1)}, bf16[256,4096]{1,0:T(8,128)(2,1)}, f32[1,256]{1,0:T(1,128)}, f32[1,2048]{1,0:T(1,128)}) custom-call(bf16[32,4096]{1,0:T(8,128)(2,1)} %rows_ref.1, bf16[2048,4096]{1,0:T(8,128)(2,1)} %table_ref.1, f32[1,2048]{1,0:T(1,128)} %bitcast.3), custom_call_target="tpu_custom_call" | custom-call | tf_op jit(solution)/shard_map/pallas_call | solution.py:284
  58.2 10.2 %shard_map.59 = (bf16[2048,4096]{1,0:T(8,128)(2,1)}, f32[1,32]{1,0:T(1,128)}, f32[1,2048]{1,0:T(1,128)}) custom-call(bf16[256,2048]{1,0:T(8,128)(2,1)} %get-tuple-element.10.weight_ref, bf16[256,4096]{1,0:T(8,128)(2,1)} %get-tuple-element.11.gathered_ref, f32[1,256]{1,0:T(1,128)} %get-tuple-element.12.duals_ref, f32[1,2048]{1,0:T(1,128)} %get-tuple-element.13.cen_ref), custom_call_target="tpu_custom_call" | custom-call | tf_op jit(solution)/shard_map/pallas_call | solution.py:318

commit v5 on v4

--- a/solution.py
+++ b/solution.py
@@ -127,7 +127,7 @@
             from_sibling.append(send(3, row, step, pair(step), columns, me_p, sibling))
 
     own.wait()
-    tile = min(width, 256)
+    tile = min(width, 1024)
 
     def accumulate(at, arrivals):
         for copy in arrivals:

time: 68.6 us -> 63.9 us (0.931)
  Pallas kernels: 67.8 us -> 63 us
    pallas_call x1, Pallas kernels: 57.6 us -> 52.8 us  [body(): pl.pallas_call(functools.partial(kernel, n_psg, n_cen), out_shape=(jax.Sh...]
where the time goes in v5:
time: 63.9 us; the launch traced here: 63.7 us
  Pallas kernels  63 us (99%)
  between operations  0.64 us (1%)
    pallas_call x1, Pallas kernels, body(): pl.pallas_call(functools.partial(kernel, n_psg, n_cen), out_shape=(jax.Sh...  52.8 us
    pallas_call x1, Pallas kernels, body(): pl.pallas_call(functools.partial(update_kernel, n_psg), grid=(width // ti...  10.2 us

profile of v5, /device:TPU:0, one launch (start us, length us, event | category | flops | bytes accessed | tf_op | source)
XLA Modules:
  0.0 63.7 jit_solution(6128604329525964125)
XLA Ops:
  0.6 52.8 %shard_map.58 = (bf16[256,2048]{1,0:T(8,128)(2,1)}, bf16[256,4096]{1,0:T(8,128)(2,1)}, f32[1,256]{1,0:T(1,128)}, f32[1,2048]{1,0:T(1,128)}) custom-call(bf16[32,4096]{1,0:T(8,128)(2,1)} %rows_ref.1, bf16[2048,4096]{1,0:T(8,128)(2,1)} %table_ref.1, f32[1,2048]{1,0:T(1,128)} %bitcast.3), custom_call_target="tpu_custom_call" | custom-call | tf_op jit(solution)/shard_map/pallas_call | solution.py:284
  53.5 10.2 %shard_map.59 = (bf16[2048,4096]{1,0:T(8,128)(2,1)}, f32[1,32]{1,0:T(1,128)}, f32[1,2048]{1,0:T(1,128)}) custom-call(bf16[256,2048]{1,0:T(8,128)(2,1)} %get-tuple-element.10.weight_ref, bf16[256,4096]{1,0:T(8,128)(2,1)} %get-tuple-element.11.gathered_ref, f32[1,256]{1,0:T(1,128)} %get-tuple-element.12.duals_ref, f32[1,2048]{1,0:T(1,128)} %get-tuple-element.13.cen_ref), custom_call_target="tpu_custom_call" | custom-call | tf_op jit(solution)/shard_map/pallas_call | solution.py:318
